TPU v7x, 32 devices: a whole 2x2x4 slice. The times are simulated.
32 devices in a mesh: groups: 2 (over y), ctx: 4 (over z), head: 2 (over x), role: 2 (over core).
Axes of the slice: x: 2, y: 2, z: 4, core: 2. Of those that a mesh axis runs over, the one named last changes fastest.
Arguments:
- prompt_query: bfloat16 [768, 64, 192], P(('groups', 'ctx'), ('head', 'role')), parts along dimension 0, may hold values from -200 to 200
- prompt_latent: bfloat16 [768, 576], P(('groups', 'ctx')), parts along dimension 0, may hold values from -60 to 60
- block_order: int32 [8], P('groups'), parts along dimension 0, may hold values from 0 to 3, as said below
- key_up: bfloat16 [64, 128, 512], P(('head', 'role')), may hold values from -0.5 to 0.5
- value_up: bfloat16 [64, 512, 128], P(('head', 'role')), may hold values from -1.796875 to 1.796875
- out_weight: bfloat16 [8192, 7168], P(('head', 'role'), 'ctx'), may hold values from -0.0625 to 0.0625
- step_query: bfloat16 [4, 8, 64, 192], P(None, 'groups', ('head', 'role')), parts along dimension 1, may hold values from -200 to 200
- cache_latent: bfloat16 [8, 1536, 576], P('groups', 'ctx'), parts along dimension 0, may hold values from -60 to 60
- step_latent: bfloat16 [4, 8, 576], P(None, 'groups'), parts along dimension 1, may hold values from -5 to 5
- cache_length: int32 [8], P('groups'), parts along dimension 0, may hold values from 2 to 1536
- block_dest: int32 [8], P('groups'), parts along dimension 0, may hold values from 0 to 3
Outputs:
- prompt_out: bfloat16 [768, 8192], P(('groups', 'ctx'), ('head', 'role')), parts along dimension 0
- step_out: bfloat16 [4, 8, 7168], P(None, 'groups', ('ctx', 'head', 'role')), parts along dimension 1
There are 2 independent parts, one for each index of `groups`. A program takes and returns all parts, laid end to end along the dimension named above; an argument that names none is the same for every part. Nothing has to cross between parts.
Inputs may be any that keep to these rules, and one draw needn't show every extreme that they name: `block_order`: a permutation: each block position appears once.
All inputs are finite; a program needn't handle non-finite values.
Results may differ from a plain program's by a relative error of at most 0.039.
Values may be sent and summed in bfloat16 or wider, within the bound.
A program may use at most 64 MiB of HBM per device.

v0:
```python
import functools
import math

import jax
import jax.numpy as jnp
from jax import lax
from jax.experimental import pallas as pl
from jax.experimental.pallas import tpu as pltpu
from jax.sharding import PartitionSpec as P

MESH = pl.DeviceIdType.MESH
LOW = -1e30


def nt_dot(a, b):
    return lax.dot_general(a, b, (((1,), (1,)), ((), ())), preferred_element_type=jnp.float32)


def nn_dot(a, b):
    return jnp.dot(a, b, preferred_element_type=jnp.float32)


def quotient(x, n):
    return x >> (n.bit_length() - 1) if n & (n - 1) == 0 else lax.div(x, n)


def remainder(x, n):
    return x & (n - 1) if n & (n - 1) == 0 else lax.rem(x, n)


def one_hot_rows(count, source):
    out_row = lax.broadcasted_iota(jnp.int32, (count, count), 0)
    in_row = lax.broadcasted_iota(jnp.int32, (count, count), 1)
    return (in_row == source(out_row)).astype(jnp.bfloat16)


def kernel(
    size,
    order_ref, length_ref, dest_ref,
    pq_hbm, pl_hbm, ku_hbm, vu_hbm, ow_hbm, sq_hbm, cache_hbm, sl_ref,
    prompt_hbm, step_ref,
    pq, ku, vu, ow, sq, cache, own, keys, query, absorbed, step_rows, sums, stats, partials, flat, parts, landed,
    prompt, prompt_sem, local_sem, lat_send, lat_recv, fwd_send, fwd_recv, part_send, part_recv, stat_send, stat_recv, out_send, out_recv,
):
    n_ctx, n_head, n_role = size["ctx"], size["head"], size["role"]
    plane = n_head * n_role
    tokens, heads, nope, latent = size["tokens"], size["heads"], size["nope"], size["latent"]
    steps, rows, span, vdim = size["steps"], size["rows"], size["span"], size["vdim"]
    made = steps * rows
    half = tokens // n_role
    scale = (size["width"] ** -0.5) * math.log2(math.e)
    place, role = lax.axis_index("ctx"), lax.axis_index("role")
    here = lax.axis_index("head") * n_role + role

    def ctx_peer(k):
        return {"ctx": lax.rem(place + k, n_ctx)}

    def plane_peer(k):
        other = lax.rem(here + k, plane)
        return {"head": lax.div(other, n_role), "role": lax.rem(other, n_role)}

    started = iter(range(local_sem.shape[0]))

    def load(src, dst, pieces=1):
        copies = []
        step = src.shape[0] // pieces
        for i in range(pieces):
            part = pl.ds(i * step, step)
            copy = pltpu.make_async_copy(src.at[part], dst.at[part], local_sem.at[next(started)])
            copy.start()
            copies.append(copy)
        return copies

    (own_copy,) = load(pl_hbm, own)
    (sq_copy,) = load(sq_hbm, sq)
    pq_copies = load(pq_hbm, pq, 2)
    ku_copies = load(ku_hbm, ku, 4)
    cache_copies = load(cache_hbm, cache, rows)
    vu_copies = load(vu_hbm, vu, 4)
    ow_copies = load(ow_hbm, ow, 8)

    barrier = pltpu.get_barrier_semaphore()
    for k in range(1, n_ctx):
        pl.semaphore_signal(barrier, inc=1, device_id=ctx_peer(k), device_id_type=MESH)
    for k in range(1, plane):
        pl.semaphore_signal(barrier, inc=1, device_id=plane_peer(k), device_id_type=MESH)

    tile = 16

    def prompt_row(r):
        return remainder(r, tile) * heads + quotient(r, tile)

    def step_row(r):
        within = remainder(r, made)
        return (remainder(within, steps) * rows + quotient(within, steps)) * heads + quotient(r, made)

    sq_copy.wait()
    moved = nn_dot(one_hot_rows(made * heads, step_row), sq[...]).astype(jnp.bfloat16)
    query[:, tokens:, :] = moved.reshape(heads, made, size["width"])
    perm = one_hot_rows(tile * heads, prompt_row)
    for copy in pq_copies:
        copy.wait()
    for i in range(tokens // tile):
        moved = nn_dot(perm, pq[i * tile * heads : (i + 1) * tile * heads, :]).astype(jnp.bfloat16)
        query[:, i * tile : (i + 1) * tile, :] = moved.reshape(heads, tile, size["width"])

    pl.semaphore_wait(barrier, n_ctx - 1 + plane - 1)

    own_copy.wait()
    keys[pl.ds(pl.multiple_of(place * tokens, 16), tokens), :] = own[...]
    my_half = pl.multiple_of(role * half, 16)
    lat_copies = []
    for k in range(1, n_ctx):
        copy = pltpu.make_async_remote_copy(
            src_ref=own.at[pl.ds(my_half, half)],
            dst_ref=keys.at[pl.ds(pl.multiple_of(place * tokens + role * half, 16), half)],
            send_sem=lat_send.at[k], recv_sem=lat_recv.at[k],
            device_id=ctx_peer(k), device_id_type=MESH,
        )
        copy.start()
        lat_copies.append(copy)

    for h in range(heads):
        if h % (heads // 4) == 0:
            ku_copies[h // (heads // 4)].wait()
        low = nn_dot(query[h, :, :nope], ku[h]).astype(jnp.bfloat16)
        absorbed[h * tokens : (h + 1) * tokens, :latent] = low[:tokens]
        absorbed[h * tokens : (h + 1) * tokens, latent:] = query[h, :tokens, nope:]
        step_low = low[tokens:].astype(jnp.float32)
        step_high = query[h, tokens:, nope:].astype(jnp.float32)
        for b in range(rows):
            step_rows[b, h * steps : (h + 1) * steps, :latent] = step_low[b * steps : (b + 1) * steps]
            step_rows[b, h * steps : (h + 1) * steps, latent:] = step_high[b * steps : (b + 1) * steps]

    each = heads * steps
    count = rows * each
    row_id = lax.broadcasted_iota(jnp.int32, (count, 1), 0)
    row_step, row_request = remainder(row_id, steps), quotient(row_id, each)
    step_q = step_rows[...].astype(jnp.bfloat16)
    flat_q = step_q.reshape(count, step_q.shape[2])
    fresh = jnp.concatenate([sl_ref[u].astype(jnp.float32) for u in range(steps)], axis=0).astype(jnp.bfloat16)
    fresh_id = lax.broadcasted_iota(jnp.int32, (1, made), 1)
    fresh_mask = (remainder(fresh_id, rows) == row_request) & (quotient(fresh_id, rows) <= row_step) & (place == 0)
    fresh_scores = jnp.where(fresh_mask, nt_dot(flat_q, fresh) * scale, LOW)
    own_scores = jnp.where(row_request == dest_ref[place], nt_dot(flat_q, own[...]) * scale, LOW)
    for copy in cache_copies:
        copy.wait()
    cache_pos = place * span + lax.broadcasted_iota(jnp.int32, (1, span), 1)
    cache_scores = jnp.concatenate(
        [jnp.where(cache_pos < length_ref[b], nn_dot(step_q[b], cache[b]) * scale, LOW) for b in range(rows)], axis=0
    )
    peak = functools.reduce(
        jnp.maximum, [jnp.max(x, axis=1, keepdims=True) for x in (cache_scores, own_scores, fresh_scores)]
    )
    cache_w, own_w, fresh_w = (jnp.exp2(x - peak) for x in (cache_scores, own_scores, fresh_scores))
    amount = functools.reduce(jnp.add, [jnp.sum(x, axis=1, keepdims=True) for x in (cache_w, own_w, fresh_w)])
    cache_w = cache_w.astype(jnp.bfloat16)
    summed = nn_dot(own_w.astype(jnp.bfloat16), own[:, :latent]) + nn_dot(
        fresh_w.astype(jnp.bfloat16), fresh[:, :latent]
    )
    for b in range(rows):
        sums[b] = summed[b * each : (b + 1) * each] + nt_dot(
            cache_w[b * each : (b + 1) * each], cache[b, :latent, :]
        )
    lane = lax.broadcasted_iota(jnp.int32, (1, 128), 1)
    at_head = lane == quotient(remainder(row_id, each), steps)

    def by_head(column, other):
        spread = jnp.where(at_head, column, 0.0).reshape(rows, each // 8, 8, 128).sum(axis=1)
        table = jnp.concatenate(
            [
                functools.reduce(jnp.add, [spread[b, j : j + steps] for j in range(0, 8, steps)])
                for b in range(rows)
            ],
            axis=0,
        )
        return jnp.where(lane < heads, table, other)

    stats[0, :made] = by_head(peak, 0.0)
    stats[0, made:] = by_head(amount, 1.0)
    for h in range(heads):
        if h % (heads // 4) == 0:
            vu_copies[h // (heads // 4)].wait()
        mine = jnp.concatenate([sums[b, h * steps : (h + 1) * steps, :] for b in range(rows)], axis=0)
        partials[0, :, h * vdim : (h + 1) * vdim] = nn_dot(mine.astype(jnp.bfloat16), vu[h]).astype(jnp.bfloat16)
    part_copies = []
    for k in range(1, n_ctx):
        for src, send, recv in ((stats, stat_send, stat_recv), (partials, part_send, part_recv)):
            copy = pltpu.make_async_remote_copy(
                src_ref=src.at[0], dst_ref=src.at[k], send_sem=send.at[k], recv_sem=recv.at[k],
                device_id=ctx_peer(k), device_id_type=MESH,
            )
            copy.start()
            part_copies.append(copy)

    fwd_copies = []
    for k in range(1, n_ctx):
        lat_copies[k - 1].wait_recv()
        source = lax.rem(place + n_ctx - k, n_ctx)
        piece = keys.at[pl.ds(pl.multiple_of(source * tokens + role * half, 16), half)]
        for j in range(1, n_role):
            copy = pltpu.make_async_remote_copy(
                src_ref=piece, dst_ref=piece, send_sem=fwd_send.at[k, j], recv_sem=fwd_recv.at[k, j],
                device_id={"role": lax.rem(role + j, n_role)}, device_id_type=MESH,
            )
            copy.start()
            fwd_copies.append(copy)

    for copy in fwd_copies:
        copy.wait_recv()
    seq = n_ctx * tokens
    key_id = lax.broadcasted_iota(jnp.int32, (1, seq), 1)
    key_pos = jnp.zeros((1, seq), jnp.int32)
    for k in range(n_ctx):
        inside = (key_id >= k * tokens) & (key_id < (k + 1) * tokens)
        key_pos = jnp.where(inside, order_ref[k] * tokens + key_id - k * tokens, key_pos)
    query_pos = order_ref[place] * tokens + lax.broadcasted_iota(jnp.int32, (tokens, 1), 0)
    bias = jnp.where(key_pos <= query_pos, 0.0, LOW).astype(jnp.float32)
    group = size["group"]

    def prompt_scores(g):
        return nt_dot(absorbed[g * group * tokens : (g + 1) * group * tokens, :], keys[...])

    prompt_copies = []

    def prompt_finish(g, s):
        s = (s * scale).reshape(group, tokens, seq) + bias[None]
        w = jnp.exp2(s - jnp.max(s, axis=2, keepdims=True))
        inverse = 1.0 / jnp.sum(w, axis=2, keepdims=True)
        o = nn_dot(w.astype(jnp.bfloat16).reshape(group * tokens, seq), keys[:, :latent])
        attended = (o.reshape(group, tokens, latent) * inverse).astype(jnp.bfloat16)
        for i in range(group):
            h = g * group + i
            prompt[:, h * vdim : (h + 1) * vdim] = nn_dot(attended[i], vu[h]).astype(jnp.bfloat16)
        cols = slice(g * group * vdim, (g + 1) * group * vdim)
        copy = pltpu.make_async_copy(prompt.at[:, cols], prompt_hbm.at[:, cols], prompt_sem.at[g])
        copy.start()
        prompt_copies.append(copy)

    n_groups = heads // group
    first = n_groups // 2
    ahead = prompt_scores(0)
    for g in range(first):
        current, ahead = ahead, prompt_scores(g + 1)
        prompt_finish(g, current)

    for copy in part_copies:
        copy.wait_recv()
    top = stats[0, :made]
    for k in range(1, n_ctx):
        top = jnp.maximum(top, stats[k, :made])
    factors = [jnp.exp2(stats[k, :made] - top) for k in range(n_ctx)]
    whole = functools.reduce(jnp.add, [factors[k] * stats[k, made:] for k in range(n_ctx)])
    factors = [f / whole for f in factors]
    for h in range(heads):
        cols = slice(h * vdim, (h + 1) * vdim)
        merged = functools.reduce(
            jnp.add, [partials[k, :, cols].astype(jnp.float32) * factors[k][:, h : h + 1] for k in range(n_ctx)]
        )
        flat[:, cols] = merged.astype(jnp.bfloat16)
    for copy in ow_copies:
        copy.wait()
    in_order = one_hot_rows(made, lambda r: remainder(r, rows) * steps + quotient(r, rows))
    projected = nn_dot(nn_dot(in_order, flat[...]).astype(jnp.bfloat16), ow[...])
    width = projected.shape[1] // plane
    for d in range(plane):
        parts[d] = projected[:, d * width : (d + 1) * width]
    out_copies = []
    for k in range(1, plane):
        copy = pltpu.make_async_remote_copy(
            src_ref=parts.at[lax.rem(here + k, plane)], dst_ref=landed.at[k],
            send_sem=out_send.at[k], recv_sem=out_recv.at[k],
            device_id=plane_peer(k), device_id_type=MESH,
        )
        copy.start()
        out_copies.append(copy)

    for g in range(first, n_groups):
        current, ahead = ahead, prompt_scores(g + 1) if g + 1 < n_groups else None
        prompt_finish(g, current)

    result = parts[here]
    for k in range(1, plane):
        out_copies[k - 1].wait_recv()
        result = result + landed[k]
    step_ref[...] = result
    for copy in lat_copies + fwd_copies + part_copies + out_copies:
        copy.wait_send()
    for copy in prompt_copies:
        copy.wait()


def write_results(prompt_in, step_in, prompt_out, step_out):
    prompt_out[...] = prompt_in[...]
    steps, rows = step_out.shape[:2]
    for t in range(steps):
        step_out[t] = step_in[t * rows : (t + 1) * rows, :].astype(step_out.dtype)


def per_device(
    prompt_query, prompt_latent, block_order, key_up, value_up, out_weight,
    step_query, cache_latent, step_latent, cache_length, block_dest,
):
    tokens, heads, width = prompt_query.shape
    nope, latent = key_up.shape[1:]
    vdim = value_up.shape[2]
    steps, rows = step_query.shape[:2]
    span, key_width = cache_latent.shape[1:]
    model = out_weight.shape[1]
    n_ctx, n_head, n_role = (lax.axis_size(a) for a in ("ctx", "head", "role"))
    plane, made, seq = n_head * n_role, steps * rows, n_ctx * tokens
    group = 4 if heads % 4 == 0 and seq <= 512 else 1
    size = dict(
        ctx=n_ctx, head=n_head, role=n_role, tokens=tokens, heads=heads, width=width, nope=nope,
        latent=latent, vdim=vdim, steps=steps, rows=rows, span=span, group=group,
    )
    bf16, f32 = jnp.bfloat16, jnp.float32
    smem, anywhere, vmem = (pl.BlockSpec(memory_space=m) for m in (pltpu.SMEM, pl.ANY, pltpu.VMEM))
    dma = pltpu.SemaphoreType.DMA
    prompt_made, step_made = pl.pallas_call(
        functools.partial(kernel, size),
        out_shape=(
            jax.ShapeDtypeStruct((tokens, heads * vdim), bf16),
            jax.ShapeDtypeStruct((made, model // plane), f32),
        ),
        in_specs=[smem] * 3 + [anywhere] * 7 + [vmem],
        out_specs=(anywhere, vmem),
        scratch_shapes=[
            pltpu.VMEM((tokens * heads, width), bf16),
            pltpu.VMEM(key_up.shape, bf16),
            pltpu.VMEM(value_up.shape, bf16),
            pltpu.VMEM(out_weight.shape, bf16),
            pltpu.VMEM((made * heads, width), bf16),
            pltpu.VMEM((rows, key_width, span), bf16),
            pltpu.VMEM((tokens, key_width), bf16),
            pltpu.VMEM((seq, key_width), bf16),
            pltpu.VMEM((heads, tokens + made, width), bf16),
            pltpu.VMEM((heads * tokens, key_width), bf16),
            pltpu.VMEM((rows, heads * steps, key_width), f32),
            pltpu.VMEM((rows, heads * steps, latent), f32),
            pltpu.VMEM((n_ctx, 2 * made, 128), f32),
            pltpu.VMEM((n_ctx, made, heads * vdim), bf16),
            pltpu.VMEM((made, heads * vdim), bf16),
            pltpu.VMEM((plane, made, model // plane), f32),
            pltpu.VMEM((plane, made, model // plane), f32),
            pltpu.VMEM((tokens, heads * vdim), bf16),
            dma((heads // group,)),
            dma((20 + rows,)),
            dma((n_ctx,)), dma((n_ctx,)),
            dma((n_ctx, n_role)), dma((n_ctx, n_role)),
            dma((n_ctx,)), dma((n_ctx,)),
            dma((n_ctx,)), dma((n_ctx,)),
            dma((plane,)), dma((plane,)),
        ],
        compiler_params=pltpu.CompilerParams(
            collective_id=0, has_side_effects=True, vmem_limit_bytes=56 * 1024 * 1024
        ),
    )(
        block_order, cache_length, block_dest,
        prompt_query.reshape(tokens * heads, width), prompt_latent, key_up, value_up, out_weight,
        step_query.reshape(made * heads, width), jnp.swapaxes(cache_latent, 1, 2), step_latent,
    )
    return pl.pallas_call(
        write_results,
        out_shape=(
            jax.ShapeDtypeStruct((tokens, heads * vdim), bf16),
            jax.ShapeDtypeStruct((steps, rows, model // plane), bf16),
        ),
        in_specs=[vmem, vmem],
        out_specs=(vmem, vmem),
        compiler_params=pltpu.CompilerParams(vmem_limit_bytes=56 * 1024 * 1024),
    )(prompt_made, step_made)


def solution(mesh):
    return jax.shard_map(
        per_device,
        mesh=mesh,
        in_specs=(
            P(("groups", "ctx"), ("head", "role"), None),
            P(("groups", "ctx"), None),
            P("groups"),
            P(("head", "role"), None, None),
            P(("head", "role"), None, None),
            P(("head", "role"), "ctx"),
            P(None, "groups", ("head", "role"), None),
            P("groups", "ctx", None),
            P(None, "groups", None),
            P("groups"),
            P("groups"),
        ),
        out_specs=(
            P(("groups", "ctx"), ("head", "role")),
            P(None, "groups", ("ctx", "head", "role")),
        ),
        check_vma=False,
    )
```

profile of v0, /device:TPU:0, one launch (start us, length us, event | category | flops | bytes accessed | tf_op | source)
XLA Modules:
  0.0 27.3 jit_solution(12052915302403128596)
XLA Ops:
  0.6 24.9 %shard_map.122 = (bf16[96,2048]{1,0:T(8,128)(2,1)}, f32[16,448]{1,0:T(8,128)}) custom-call(s32[4]{0:T(128)} %order_ref.1, s32[4]{0:T(128)} %length_ref.1, s32[4]{0:T(128)} %dest_ref.1, bf16[1536,192]{1,0:T(8,128)(2,1)} %bitcast.4, bf16[96,576]{1,0:T(8,128)(2,1)} %pl_hbm.1, bf16[16,128,512]{2,1,0:T(8,128)(2,1)} %ku_hbm.1, bf16[16,512,128]{2,1,0:T(8,128)(2,1)} %vu_hbm.1, ...), custom_call_target="tpu_custom_call" | custom-call | tf_op jit(solution)/shard_map/pallas_call | solution.py:320
  25.5 1.8 %shard_map.123 = (bf16[96,2048]{1,0:T(8,128)(2,1)}, bf16[4,4,448]{2,1,0:T(4,128)(2,1)}) custom-call(bf16[96,2048]{1,0:T(8,128)(2,1)} %get-tuple-element.4.prompt_in, f32[16,448]{1,0:T(8,128)} %get-tuple-element.5.step_in), custom_call_target="tpu_custom_call" | custom-call | tf_op jit(solution)/shard_map/pallas_call | solution.py:363
where the time goes:
time: 27.5 us; the launch traced here: 27.3 us
  Pallas kernels  26.6 us (97%)
  between operations  0.64 us (2%)
    pallas_call x1, Pallas kernels, per_device(): pl.pallas_call(functools.partial(kernel, size), out_shape=(jax.ShapeDtype...  24.9 us
    pallas_call x1, Pallas kernels, per_device(): pl.pallas_call(write_results, out_shape=(jax.ShapeDtypeStruct((tokens, he...  1.77 us

commit v1 on v0

--- a/solution.py
+++ b/solution.py
@@ -39,8 +39,8 @@
     order_ref, length_ref, dest_ref,
     pq_hbm, pl_hbm, ku_hbm, vu_hbm, ow_hbm, sq_hbm, cache_hbm, sl_ref,
     prompt_hbm, step_ref,
-    pq, ku, vu, ow, sq, cache, own, keys, query, absorbed, step_rows, sums, stats, partials, flat, parts, landed,
-    prompt, prompt_sem, local_sem, lat_send, lat_recv, fwd_send, fwd_recv, part_send, part_recv, stat_send, stat_recv, out_send, out_recv,
+    pq, ku, vu, ow, sq, cache, own, keys, query, absorbed, step_rows, sums, stats, part_out, part_in, flat, parts, landed,
+    prompt, prompt_sem, local_sem, lat_send, lat_recv, fwd_send, fwd_recv, part_send, part_recv, stat_send, stat_recv, flat_send, flat_recv, out_send, out_recv,
 ):
     n_ctx, n_head, n_role = size["ctx"], size["head"], size["role"]
     plane = n_head * n_role
@@ -51,6 +51,9 @@
     scale = (size["width"] ** -0.5) * math.log2(math.e)
     place, role = lax.axis_index("ctx"), lax.axis_index("role")
     here = lax.axis_index("head") * n_role + role
+    shares = size["shares"]
+    per = heads // shares
+    mine_at = place if shares > 1 else 0
 
     def ctx_peer(k):
         return {"ctx": lax.rem(place + k, n_ctx)}
@@ -84,25 +87,6 @@
         pl.semaphore_signal(barrier, inc=1, device_id=ctx_peer(k), device_id_type=MESH)
     for k in range(1, plane):
         pl.semaphore_signal(barrier, inc=1, device_id=plane_peer(k), device_id_type=MESH)
-
-    tile = 16
-
-    def prompt_row(r):
-        return remainder(r, tile) * heads + quotient(r, tile)
-
-    def step_row(r):
-        within = remainder(r, made)
-        return (remainder(within, steps) * rows + quotient(within, steps)) * heads + quotient(r, made)
-
-    sq_copy.wait()
-    moved = nn_dot(one_hot_rows(made * heads, step_row), sq[...]).astype(jnp.bfloat16)
-    query[:, tokens:, :] = moved.reshape(heads, made, size["width"])
-    perm = one_hot_rows(tile * heads, prompt_row)
-    for copy in pq_copies:
-        copy.wait()
-    for i in range(tokens // tile):
-        moved = nn_dot(perm, pq[i * tile * heads : (i + 1) * tile * heads, :]).astype(jnp.bfloat16)
-        query[:, i * tile : (i + 1) * tile, :] = moved.reshape(heads, tile, size["width"])
 
     pl.semaphore_wait(barrier, n_ctx - 1 + plane - 1)
 
@@ -119,6 +103,25 @@
         )
         copy.start()
         lat_copies.append(copy)
+
+    tile = 16
+
+    def prompt_row(r):
+        return remainder(r, tile) * heads + quotient(r, tile)
+
+    def step_row(r):
+        within = remainder(r, made)
+        return (remainder(within, steps) * rows + quotient(within, steps)) * heads + quotient(r, made)
+
+    sq_copy.wait()
+    moved = nn_dot(one_hot_rows(made * heads, step_row), sq[...]).astype(jnp.bfloat16)
+    query[:, tokens:, :] = moved.reshape(heads, made, size["width"])
+    perm = one_hot_rows(tile * heads, prompt_row)
+    for copy in pq_copies:
+        copy.wait()
+    for i in range(tokens // tile):
+        moved = nn_dot(perm, pq[i * tile * heads : (i + 1) * tile * heads, :]).astype(jnp.bfloat16)
+        query[:, i * tile : (i + 1) * tile, :] = moved.reshape(heads, tile, size["width"])
 
     for h in range(heads):
         if h % (heads // 4) == 0:
@@ -163,31 +166,28 @@
             cache_w[b * each : (b + 1) * each], cache[b, :latent, :]
         )
     lane = lax.broadcasted_iota(jnp.int32, (1, 128), 1)
-    at_head = lane == quotient(remainder(row_id, each), steps)
-
-    def by_head(column, other):
-        spread = jnp.where(at_head, column, 0.0).reshape(rows, each // 8, 8, 128).sum(axis=1)
-        table = jnp.concatenate(
-            [
-                functools.reduce(jnp.add, [spread[b, j : j + steps] for j in range(0, 8, steps)])
-                for b in range(rows)
-            ],
-            axis=0,
-        )
-        return jnp.where(lane < heads, table, other)
-
-    stats[0, :made] = by_head(peak, 0.0)
-    stats[0, made:] = by_head(amount, 1.0)
+    row_head = quotient(remainder(row_id, each), steps)
+    spread = jnp.where(lane == row_head, peak, jnp.where(lane == 64 + row_head, amount, 0.0))
+    spread = spread.reshape(rows, each // 8, 8, 128).sum(axis=1)
+    stats[0] = jnp.concatenate(
+        [functools.reduce(jnp.add, [spread[b, j : j + steps] for j in range(0, 8, steps)]) for b in range(rows)],
+        axis=0,
+    )
     for h in range(heads):
         if h % (heads // 4) == 0:
             vu_copies[h // (heads // 4)].wait()
         mine = jnp.concatenate([sums[b, h * steps : (h + 1) * steps, :] for b in range(rows)], axis=0)
-        partials[0, :, h * vdim : (h + 1) * vdim] = nn_dot(mine.astype(jnp.bfloat16), vu[h]).astype(jnp.bfloat16)
-    part_copies = []
+        at = (h % per) * vdim
+        part_out[h // per, :, at : at + vdim] = nn_dot(mine.astype(jnp.bfloat16), vu[h]).astype(jnp.bfloat16)
+    part_copies, flat_copies = [], []
     for k in range(1, n_ctx):
-        for src, send, recv in ((stats, stat_send, stat_recv), (partials, part_send, part_recv)):
+        target = lax.rem(place + k, n_ctx) if shares > 1 else 0
+        for src, dst, send, recv in (
+            (stats.at[0], stats.at[k], stat_send, stat_recv),
+            (part_out.at[target], part_in.at[k], part_send, part_recv),
+        ):
             copy = pltpu.make_async_remote_copy(
-                src_ref=src.at[0], dst_ref=src.at[k], send_sem=send.at[k], recv_sem=recv.at[k],
+                src_ref=src, dst_ref=dst, send_sem=send.at[k], recv_sem=recv.at[k],
                 device_id=ctx_peer(k), device_id_type=MESH,
             )
             copy.start()
@@ -237,31 +237,49 @@
         copy.start()
         prompt_copies.append(copy)
 
+    def merge():
+        for copy in part_copies:
+            copy.wait_recv()
+        peaks = [stats[k, :, :heads] for k in range(n_ctx)]
+        top = functools.reduce(jnp.maximum, peaks)
+        factors = [jnp.exp2(p - top) for p in peaks]
+        whole = functools.reduce(jnp.add, [factors[k] * stats[k, :, 64 : 64 + heads] for k in range(n_ctx)])
+        factors = [f / whole for f in factors]
+        head_lane = lax.broadcasted_iota(jnp.int32, (made, heads), 1)
+        pieces = []
+        for j in range(per):
+            wanted = head_lane == (place * per + j if shares > 1 else j)
+            merged = jnp.zeros((made, vdim), jnp.float32)
+            for k in range(n_ctx):
+                factor = jnp.sum(jnp.where(wanted, factors[k], 0.0), axis=1, keepdims=True)
+                cols = slice(j * vdim, (j + 1) * vdim)
+                part = part_in[k, :, cols] if k else part_out[mine_at, :, cols]
+                merged = merged + part.astype(jnp.float32) * factor
+            pieces.append(merged.astype(jnp.bfloat16))
+        in_order = one_hot_rows(made, lambda r: remainder(r, rows) * steps + quotient(r, rows))
+        flat[mine_at] = nn_dot(in_order, jnp.concatenate(pieces, axis=1)).astype(jnp.bfloat16)
+        for k in range(1, n_ctx if shares > 1 else 1):
+            copy = pltpu.make_async_remote_copy(
+                src_ref=flat.at[mine_at], dst_ref=flat.at[mine_at], send_sem=flat_send.at[k], recv_sem=flat_recv.at[k],
+                device_id=ctx_peer(k), device_id_type=MESH,
+            )
+            copy.start()
+            flat_copies.append(copy)
+
     n_groups = heads // group
-    first = n_groups // 2
+    first = max(n_groups // 2, 1)
     ahead = prompt_scores(0)
     for g in range(first):
-        current, ahead = ahead, prompt_scores(g + 1)
+        current, ahead = ahead, prompt_scores(g + 1) if g + 1 < n_groups else None
         prompt_finish(g, current)
-
-    for copy in part_copies:
+        if g == 0:
+            merge()
+
+    for copy in flat_copies:
         copy.wait_recv()
-    top = stats[0, :made]
-    for k in range(1, n_ctx):
-        top = jnp.maximum(top, stats[k, :made])
-    factors = [jnp.exp2(stats[k, :made] - top) for k in range(n_ctx)]
-    whole = functools.reduce(jnp.add, [factors[k] * stats[k, made:] for k in range(n_ctx)])
-    factors = [f / whole for f in factors]
-    for h in range(heads):
-        cols = slice(h * vdim, (h + 1) * vdim)
-        merged = functools.reduce(
-            jnp.add, [partials[k, :, cols].astype(jnp.float32) * factors[k][:, h : h + 1] for k in range(n_ctx)]
-        )
-        flat[:, cols] = merged.astype(jnp.bfloat16)
     for copy in ow_copies:
         copy.wait()
-    in_order = one_hot_rows(made, lambda r: remainder(r, rows) * steps + quotient(r, rows))
-    projected = nn_dot(nn_dot(in_order, flat[...]).astype(jnp.bfloat16), ow[...])
+    projected = nn_dot(jnp.concatenate([flat[c] for c in range(shares)], axis=1), ow[...])
     width = projected.shape[1] // plane
     for d in range(plane):
         parts[d] = projected[:, d * width : (d + 1) * width]
@@ -284,7 +302,7 @@
         out_copies[k - 1].wait_recv()
         result = result + landed[k]
     step_ref[...] = result
-    for copy in lat_copies + fwd_copies + part_copies + out_copies:
+    for copy in lat_copies + fwd_copies + part_copies + flat_copies + out_copies:
         copy.wait_send()
     for copy in prompt_copies:
         copy.wait()
@@ -309,10 +327,11 @@
     model = out_weight.shape[1]
     n_ctx, n_head, n_role = (lax.axis_size(a) for a in ("ctx", "head", "role"))
     plane, made, seq = n_head * n_role, steps * rows, n_ctx * tokens
+    shares = n_ctx if heads % n_ctx == 0 else 1
     group = 4 if heads % 4 == 0 and seq <= 512 else 1
     size = dict(
         ctx=n_ctx, head=n_head, role=n_role, tokens=tokens, heads=heads, width=width, nope=nope,
-        latent=latent, vdim=vdim, steps=steps, rows=rows, span=span, group=group,
+        latent=latent, vdim=vdim, steps=steps, rows=rows, span=span, group=group, shares=shares,
     )
     bf16, f32 = jnp.bfloat16, jnp.float32
     smem, anywhere, vmem = (pl.BlockSpec(memory_space=m) for m in (pltpu.SMEM, pl.ANY, pltpu.VMEM))
@@ -338,9 +357,10 @@
             pltpu.VMEM((heads * tokens, key_width), bf16),
             pltpu.VMEM((rows, heads * steps, key_width), f32),
             pltpu.VMEM((rows, heads * steps, latent), f32),
-            pltpu.VMEM((n_ctx, 2 * made, 128), f32),
-            pltpu.VMEM((n_ctx, made, heads * vdim), bf16),
-            pltpu.VMEM((made, heads * vdim), bf16),
+            pltpu.VMEM((n_ctx, made, 128), f32),
+            pltpu.VMEM((shares, made, heads * vdim // shares), bf16),
+            pltpu.VMEM((n_ctx, made, heads * vdim // shares), bf16),
+            pltpu.VMEM((shares, made, heads * vdim // shares), bf16),
             pltpu.VMEM((plane, made, model // plane), f32),
             pltpu.VMEM((plane, made, model // plane), f32),
             pltpu.VMEM((tokens, heads * vdim), bf16),
@@ -348,6 +368,7 @@
             dma((20 + rows,)),
             dma((n_ctx,)), dma((n_ctx,)),
             dma((n_ctx, n_role)), dma((n_ctx, n_role)),
+            dma((n_ctx,)), dma((n_ctx,)),
             dma((n_ctx,)), dma((n_ctx,)),
             dma((n_ctx,)), dma((n_ctx,)),
             dma((plane,)), dma((plane,)),

time: 27.5 us -> 27.6 us (level)
  no operation moved by 1% of the time
where the time goes in v1:
time: 27.6 us; the launch traced here: 27.5 us
  Pallas kernels  26.8 us (97%)
  between operations  0.64 us (2%)
    pallas_call x1, Pallas kernels, per_device(): pl.pallas_call(functools.partial(kernel, size), out_shape=(jax.ShapeDtype...  25 us
    pallas_call x1, Pallas kernels, per_device(): pl.pallas_call(write_results, out_shape=(jax.ShapeDtypeStruct((tokens, he...  1.77 us

profile of v1, /device:TPU:0, one launch (start us, length us, event | category | flops | bytes accessed | tf_op | source)
XLA Modules:
  0.0 27.5 jit_solution(7935979788907096449)
XLA Ops:
  0.6 25.0 %shard_map.122 = (bf16[96,2048]{1,0:T(8,128)(2,1)}, f32[16,448]{1,0:T(8,128)}) custom-call(s32[4]{0:T(128)} %order_ref.1, s32[4]{0:T(128)} %length_ref.1, s32[4]{0:T(128)} %dest_ref.1, bf16[1536,192]{1,0:T(8,128)(2,1)} %bitcast.4, bf16[96,576]{1,0:T(8,128)(2,1)} %pl_hbm.1, bf16[16,128,512]{2,1,0:T(8,128)(2,1)} %ku_hbm.1, bf16[16,512,128]{2,1,0:T(8,128)(2,1)} %vu_hbm.1, ...), custom_call_target="tpu_custom_call" | custom-call | tf_op jit(solution)/shard_map/pallas_call | solution.py:339
  25.7 1.8 %shard_map.123 = (bf16[96,2048]{1,0:T(8,128)(2,1)}, bf16[4,4,448]{2,1,0:T(4,128)(2,1)}) custom-call(bf16[96,2048]{1,0:T(8,128)(2,1)} %get-tuple-element.4.prompt_in, f32[16,448]{1,0:T(8,128)} %get-tuple-element.5.step_in), custom_call_target="tpu_custom_call" | custom-call | tf_op jit(solution)/shard_map/pallas_call | solution.py:384
